TPU v7x, 128 devices: a whole 4x4x4 slice. The times are simulated.
128 devices in a mesh: row: 32 (over z, x, core), col: 4 (over y).
Axes of the slice: x: 4, y: 4, z: 4, core: 2. Of those that a mesh axis runs over, the one named last changes fastest.
Arguments:
- gradients: bfloat16 [3, 512, 73728], P(None, 'row', 'col'), may hold values from -300 to 300
- parameter: float32 [512, 73728], P('row', 'col'), may hold values from -120 to 120
- row_state: float32 [512], P('row'), may hold values from 0.02 to 4.5, as said below
- col_state: float32 [73728], P('col'), may hold values from 0.02 to 4.5, as said below
Outputs:
- new_parameter: float32 [512, 73728], P('row', 'col')
- new_row_state: float32 [512], P('row')
- new_col_state: float32 [73728], P('col')
Inputs may be any that keep to these rules, and one draw needn't show every extreme that they name: `row_state`: positive row moments. `col_state`: positive column moments.
All inputs are finite; a program needn't handle non-finite values.
Results may differ from a plain program's by a relative error of at most 0.0003.
Values sent between devices are 32-bit elements; how exact they have to be, the bound alone decides.
A program may use at most 64 MiB of HBM per device.

v0:
```python
import functools

import jax
import jax.numpy as jnp
import numpy as np
from jax import lax
from jax.experimental import pallas as pl
from jax.experimental.pallas import tpu as pltpu
from jax.sharding import PartitionSpec as P

MESH = pl.DeviceIdType.MESH
START = 100
F32 = jnp.float32

NZ, NX, NK, NY = 4, 4, 2, 4
NROW, NALL = NZ * NX * NK, NZ * NX * NK * NY
STEPS, LROWS, LCOLS = 3, 16, 18432
ROWS, COLS = LROWS * NROW, LCOLS * NY
TILES = LCOLS // 128
HALF, HCOLS = TILES // 2, LCOLS // 2
PIECES = 8
PTILES = HALF // PIECES
PCOLS = PTILES * 128
SROWS = 32
WROWS = 56
PRODUCTS = 6
SENT = 2 * PIECES * SROWS + PIECES * WROWS + 6 * (3 * SROWS + WROWS) + NY - 1 + NALL - 1
LOADED = LROWS * TILES + HALF
OUT_PARTS = 3


def far_first():
    dist = (0, 1, 2, 1)
    offs = [(dz, dx, dy, dk) for dz in range(NZ) for dx in range(NX) for dy in range(NY) for dk in range(NK)]
    offs = [o for o in offs if o != (0, 0, 0, 0)]
    return sorted(offs, key=lambda o: (-(dist[o[0]] + dist[o[1]] + dist[o[2]]), -o[3]))


def rates():
    out = []
    for k in range(STEPS):
        t = np.float32(START + 1 + k)
        forget = np.float32(1.0) - np.power(t, np.float32(-0.8))
        out.append((float(forget), float(np.float32(1.0) - forget), float(np.power(t, np.float32(-0.5)))))
    return out


def up(x, n):
    return pltpu.roll(x, 8 - n, 0)


def down(x, n):
    return pltpu.roll(x, n, 0)


def fold8(v):
    s = lax.broadcasted_iota(jnp.int32, (8, 128), 0)
    m4, m2, m1 = s < 4, lax.rem(s, 4) < 2, lax.rem(s, 2) < 1
    w = [jnp.where(m4, v[i], v[i + 4]) + up(jnp.where(m4, v[i + 4], v[i]), 4) for i in range(4)]
    x = [jnp.where(m2, w[i] + up(w[i], 2), w[i + 2] + down(w[i + 2], 2)) for i in range(2)]
    return jnp.where(m1, x[0] + up(x[0], 1), x[1] + down(x[1], 1))


def kernel(
    grad_hbm, param_hbm, row_hbm, col_hbm,
    p, u, factor_ref, newrow_ref, newcol_ref,
    g, row_ref, col_ref, s, s_in, s_sum, r1, r2, rowbox, w, w_in, w_sum, wr, c, bbox, loaded, sent,
    g_sem, row_sem, load_sem, send, sp_r, r1_r, r2_r, box_r, wp_r, wr_r, c_r, cp_r, b_r, sem_p, sem_c, sem_d,
):
    rate = rates()
    row, y = lax.axis_index("row"), lax.axis_index("col")
    z, x, k = lax.div(row, 8), lax.rem(lax.div(row, 2), 4), lax.rem(row, 2)
    zz = [z, *[lax.rem(z + d, NZ) for d in range(1, NZ)]]
    xx = [x, *[lax.rem(x + d, NX) for d in range(1, NX)]]
    yy = [y, *[lax.rem(y + d, NY) for d in range(1, NY)]]
    kk = [k, 1 - k]

    def at(dz=0, dx=0, dy=0, dk=0):
        return (zz[dz] * 8 + xx[dx] * 2 + kk[dk], yy[dy])

    order = (2, 1, 3)
    pair = at(dk=1)
    xs = [at(dx=d) for d in order]
    zs = [at(dz=d) for d in order]
    ys = [at(dy=d) for d in order]

    def signal(sem, devices):
        for d in devices:
            pl.semaphore_signal(sem, inc=1, device_id=d, device_id_type=MESH)

    def remote(src, dst, recv, device):
        return pltpu.make_async_remote_copy(src, dst, send, recv, device_id=device, device_id_type=MESH)

    def several(ref, count, recv):
        return remote(ref.at[pl.ds(0, count)], ref.at[pl.ds(0, count)], recv, pair)

    halves = (1 - k, k)

    def columns(h):
        return pl.ds(pl.multiple_of(halves[h] * HCOLS, 128), HCOLS)

    barrier = pltpu.get_barrier_semaphore()
    g_loads = [pltpu.make_async_copy(grad_hbm.at[:, :, columns(h)], g.at[h], g_sem.at[h]) for h in range(2)]
    p_loads = [pltpu.make_async_copy(param_hbm.at[:, columns(h)], p.at[h], load_sem) for h in range(2)]
    col_load = pltpu.make_async_copy(col_hbm.at[pl.ds(pl.multiple_of(k * HALF, 8), HALF)], col_ref, load_sem)
    row_load = pltpu.make_async_copy(row_hbm, row_ref, row_sem)
    g_loads[0].start()
    signal(barrier, [(d[0] - k, d[1]) for d in (*zs, *xs, *ys)])

    @pl.when(k == 0)
    def _():
        signal(barrier, [pair])

    for load in (g_loads[1], row_load, col_load, *p_loads):
        load.start()

    lane = lax.broadcasted_iota(jnp.int32, (LROWS, 128), 1)
    sublane = lax.broadcasted_iota(jnp.int32, (LROWS, 128), 0)
    zero = jnp.zeros((8, 128), F32)

    def tile(h, i, n):
        return g[h, i, :, n * 128 : (n + 1) * 128].astype(F32)

    rows = [[None] * 4 for _ in range(STEPS)]

    def squares(h):
        g_loads[h].wait()
        for q in range(PIECES):
            last = []
            for i in range(STEPS):
                sums = []
                for j in range(PTILES):
                    a = tile(h, i, q * PTILES + j)
                    a = a * a
                    rows[i][j % 4] = a if rows[i][j % 4] is None else rows[i][j % 4] + a
                    sums.append(a[:8] + a[8:])
                s[h, q, 8 * i : 8 * i + 8, :] = fold8(sums[:8])
                last.append(sums[8])
            s[h, q, 24:32, :] = fold8(last + [zero] * (8 - STEPS))

    sp_copies = [
        remote(s.at[0, pl.ds(m * 4, 4)], s_in.at[pl.ds(m * 4, 4)], sp_r.at[m], pair) for m in range(2)
    ]
    squares(0)

    @pl.when(k == 1)
    def _():
        pl.semaphore_wait(barrier, 1)
        signal(sem_p, [pair])

    @pl.when(k == 0)
    def _():
        pl.semaphore_wait(sem_p, 1)

    for copy in sp_copies:
        copy.start()
    squares(1)

    packed = jnp.zeros((LROWS, 128), F32)
    for i in range(STEPS):
        total = (rows[i][0] + rows[i][1]) + (rows[i][2] + rows[i][3])
        packed = jnp.where(lane == sublane + LROWS * i, jnp.sum(total, axis=1, keepdims=True), packed)
    rowbox[y] = jnp.sum(packed, axis=0, keepdims=True)

    @pl.when(k == 0)
    def _():
        pl.semaphore_wait(barrier, 18)
        signal(sem_p, [pair])

    @pl.when(k == 1)
    def _():
        pl.semaphore_wait(sem_p, 1)

    for d in ys:
        remote(rowbox.at[y], rowbox.at[y], box_r, d).start()

    def scatter_x(mine, ref, recv):
        ref[x] = mine[x]
        for n, d in enumerate(order):
            remote(mine.at[xx[d]], ref.at[x], recv, xs[n]).start()

    def scatter_z(mine, ref, recv):
        ref[4 + z] = mine[4 + z]
        for n, d in enumerate(order):
            remote(mine.at[4 + zz[d]], ref.at[4 + z], recv, zs[n]).start()

    def four(ref, first=0):
        return (ref[first] + ref[first + 1]) + (ref[first + 2] + ref[first + 3])

    sp_copies[0].wait_recv()
    for q in range(4):
        s_sum[q] = s[1, q] + s_in[q]
    scatter_x(s_sum, r1, r1_r.at[0])
    sp_copies[1].wait_recv()
    for q in range(4, 8):
        s_sum[q] = s[1, q] + s_in[q]
    scatter_z(s_sum, r1, r1_r.at[1])
    signal(sem_c, xs)

    def norm(h):
        def group(n, acc):
            for j in range(8):
                a = p[h, :, pl.ds(pl.multiple_of(n * 1024 + j * 128, 128), 128)]
                a = a * a
                acc = acc + (a[:8] + a[8:])
            return acc

        return group

    psum = zero
    pltpu.make_async_copy(loaded, loaded, load_sem).wait()
    for h in range(2):
        psum = lax.fori_loop(0, HCOLS // 1024, norm(h), psum)
    pl.semaphore_wait(sem_c, 3)
    signal(sem_d, zs)

    row_load.wait()
    i0 = lax.broadcasted_iota(jnp.int32, (LROWS, LROWS), 0)
    i1 = lax.broadcasted_iota(jnp.int32, (LROWS, LROWS), 1)
    state = jnp.sum(jnp.where(i0 == i1, row_ref[...], 0.0), axis=1, keepdims=True)
    several(rowbox, 3, box_r).wait_recv()
    totals = (rowbox[0] + rowbox[1]) + (rowbox[2] + rowbox[3])
    rr = []
    for i in range(STEPS):
        total = jnp.sum(jnp.where(lane == sublane + LROWS * i, totals, 0.0), axis=1, keepdims=True)
        state = rate[i][0] * state + rate[i][1] * (total / COLS)
        rr.append(jnp.broadcast_to(lax.rsqrt(state), (LROWS, 128)))

    def products(h):
        def piece(q, _):
            sums = [[] for _ in range(PRODUCTS)]
            for j in range(PTILES):
                cols = pl.ds(pl.multiple_of(q * PCOLS + j * 128, 128), 128)
                a = [g[h, i, :, cols].astype(F32) * rr[i] for i in range(STEPS)]
                b = p[h, :, cols]
                for m, v in enumerate((a[0] * a[0], a[1] * a[1], a[2] * a[2], a[0] * a[1], a[0] * b, a[1] * b)):
                    sums[m].append(v[:8] + v[8:])
            for m in range(PRODUCTS):
                w[h, q, 8 * m : 8 * m + 8, :] = fold8(sums[m][:8])
            w[h, q, 48:56, :] = fold8([*[v[8] for v in sums], zero, zero])
            if h == 0:
                remote(w.at[0, q], w_in.at[q], wp_r.at[lax.div(q, 4)], pair).start()
            return 0

        return piece

    wp_copies = [
        remote(w.at[0, pl.ds(m * 4, 4)], w_in.at[pl.ds(m * 4, 4)], wp_r.at[m], pair) for m in range(2)
    ]
    lax.fori_loop(0, PIECES, products(0), 0)

    several(r1, 3, r1_r.at[0]).wait_recv()
    r2[z] = four(r1)
    for d in zs:
        remote(r2.at[z], r2.at[z], r2_r, d).start()
    several(r1, 3, r1_r.at[1]).wait_recv()
    r2[4 + x] = four(r1, 4)
    for d in xs:
        remote(r2.at[4 + x], r2.at[4 + x], r2_r, d).start()

    lax.fori_loop(0, 4, products(1), 0)
    wp_copies[0].wait_recv()
    for q in range(4):
        w_sum[q] = w[1, q] + w_in[q]
    scatter_x(w_sum, wr, wr_r.at[0])
    lax.fori_loop(4, 8, products(1), 0)
    wp_copies[1].wait_recv()
    for q in range(4, 8):
        w_sum[q] = w[1, q] + w_in[q]
    scatter_z(w_sum, wr, wr_r.at[1])

    scale = []
    several(r2, 6, r2_r).wait_recv()
    for axis, mine in ((0, x), (1, z + 4)):
        sums = four(r2, 4 * axis)
        first = mine * PTILES
        state8, state1 = col_ref[pl.ds(first, 8), :], col_ref[pl.ds(first + 8, 1), :]
        scale8, scale1 = [], []
        for i in range(STEPS):
            state8 = rate[i][0] * state8 + rate[i][1] * (sums[8 * i : 8 * i + 8] / ROWS)
            state1 = rate[i][0] * state1 + rate[i][1] * (sums[24 + i : 25 + i] / ROWS)
            c[1, mine, 8 * i : 8 * i + 8, :] = state8
            c[1, mine, 24 + i : 25 + i, :] = state1
            scale8.append(lax.rsqrt(state8))
            scale1.append(lax.rsqrt(state1))
        scale.append((scale8, scale1))
        for d in zs if axis else xs:
            remote(c.at[1, mine], c.at[1, mine], c_r, d).start()

    acc = [None] * PRODUCTS
    extra = None
    for axis in range(2):
        several(wr, 3, wr_r.at[axis]).wait_recv()
        sums = four(wr, 4 * axis)
        q8, q1 = scale[axis]
        for m, f in enumerate((q8[0] * q8[0], q8[1] * q8[1], q8[2] * q8[2], q8[0] * q8[1], q8[0], q8[1])):
            v = f * sums[8 * m : 8 * m + 8]
            acc[m] = v if axis == 0 else acc[m] + v
        f = (q1[0] * q1[0], q1[1] * q1[1], q1[2] * q1[2], q1[0] * q1[1], q1[0], q1[1], q1[0] * 0.0, q1[0] * 0.0)
        v = jnp.concatenate(f, axis=0) * sums[48:56]
        extra = v if axis == 0 else extra + v
    sums = jnp.sum(fold8([*acc, psum, zero]) + extra, axis=1, keepdims=True)
    j0 = lax.broadcasted_iota(jnp.int32, (8, 128), 0)
    j1 = lax.broadcasted_iota(jnp.int32, (8, 128), 1)
    me = y * NROW + row
    bbox[me] = jnp.sum(jnp.where(j0 == j1, sums, 0.0), axis=0, keepdims=True)
    pl.semaphore_wait(sem_d, 3)
    for off in far_first():
        remote(bbox.at[me], bbox.at[me], b_r, at(*off)).start()

    newrow_ref[...] = jnp.sum(jnp.where(i0 == i1, state, 0.0), axis=0, keepdims=True)

    def updates(h):
        def piece(q, _):
            scales = lax.rsqrt(c[h, q])
            for j in range(PTILES):
                cols = pl.ds(pl.multiple_of(q * PCOLS + j * 128, 128), 128)
                for i in range(STEPS):
                    at_row = 8 * i + j if j < 8 else 24 + i
                    u[h, i, :, cols] = g[h, i, :, cols].astype(F32) * rr[i] * scales[at_row : at_row + 1]
            return 0

        return piece

    c_copy = remote(c.at[1], c.at[0], cp_r, pair)
    several(c.at[1], 6, c_r).wait_recv()
    c_copy.start()
    for h in (1, 0):
        if h == 0:
            c_copy.wait_recv()
        lax.fori_loop(0, PIECES, updates(h), 0)
        for q in range(PIECES):
            newcol_ref[h, q * PTILES : q * PTILES + 8, :] = c[h, q, 16:24, :]
            newcol_ref[h, q * PTILES + 8 : q * PTILES + 9, :] = c[h, q, 26:27, :]

    several(bbox, NALL - 1, b_r).wait_recv()
    sums = [bbox[i] for i in range(NALL)]
    while len(sums) > 1:
        sums = [sums[i] + sums[i + 1] for i in range(0, len(sums), 2)]
    sums = sums[0]
    j1 = lax.broadcasted_iota(jnp.int32, (1, 128), 1)
    uu0, uu1, uu2, u01, pu0, pu1, pp = [
        jnp.sum(jnp.where(j1 == m, sums, 0.0), axis=1, keepdims=True) for m in range(7)
    ]
    count = float(ROWS * COLS)
    clip = [jnp.minimum(1.0, lax.rsqrt(v * (1.0 / count))) for v in (uu0, uu1, uu2)]
    f0 = rate[0][2] * clip[0] * jnp.sqrt(pp * (1.0 / count))
    pp = pp - 2.0 * f0 * pu0 + f0 * f0 * uu0
    f1 = rate[1][2] * clip[1] * jnp.sqrt(pp * (1.0 / count))
    pp = pp - 2.0 * f1 * (pu1 - f0 * u01) + f1 * f1 * uu1
    f2 = rate[2][2] * clip[2] * jnp.sqrt(pp * (1.0 / count))
    for i, v in enumerate((f0, f1, f2)):
        factor_ref[i] = jnp.broadcast_to(v, (8, 128))

    remote(sent, sent, b_r, pair).wait_send()


def finish(p, u, factor_ref, newrow_ref, newcol_ref, out_hbm, row_hbm, col_hbm, o, written, out_sem, row_sem):
    k = lax.rem(lax.axis_index("row"), 2)
    halves = (1 - k, k)
    outs = [pltpu.make_async_copy(newrow_ref, row_hbm, row_sem)]
    for h in range(2):
        tiles = pl.ds(pl.multiple_of(halves[h] * HALF, 8), HALF)
        outs.append(pltpu.make_async_copy(newcol_ref.at[h], col_hbm.at[tiles], out_sem))
    for out in outs:
        out.start()
    f = [jnp.concatenate([factor_ref[i], factor_ref[i]], axis=0) for i in range(STEPS)]
    width = HCOLS // OUT_PARTS
    for h in range(2):
        for part in range(OUT_PARTS):
            for n in range(width // 128):
                cols = pl.ds(part * width + n * 128, 128)
                a = p[h, :, cols] - f[0] * u[h, 0, :, cols]
                o[h, :, cols] = a - (f[1] * u[h, 1, :, cols] + f[2] * u[h, 2, :, cols])
            src = o.at[h, :, pl.ds(part * width, width)]
            dst = out_hbm.at[:, pl.ds(pl.multiple_of(halves[h] * HCOLS + part * width, 128), width)]
            pltpu.make_async_copy(src, dst, out_sem).start()
    outs[0].wait()
    pltpu.make_async_copy(written, written, out_sem).wait()


def local(gradients, parameter, row_state, col_state):
    args = (gradients, parameter, row_state.reshape(1, LROWS), col_state.reshape(TILES, 128))
    vmem = pl.BlockSpec(memory_space=pltpu.VMEM)
    hbm = pl.BlockSpec(memory_space=pltpu.HBM)
    dma = pltpu.SemaphoreType.DMA
    regular, two = pltpu.SemaphoreType.REGULAR, dma((2,))
    state = pl.pallas_call(
        kernel,
        name="exchange",
        out_shape=(
            jax.ShapeDtypeStruct((2, LROWS, HCOLS), F32),
            jax.ShapeDtypeStruct((2, STEPS, LROWS, HCOLS), F32),
            jax.ShapeDtypeStruct((STEPS, 8, 128), F32),
            jax.ShapeDtypeStruct((1, LROWS), F32),
            jax.ShapeDtypeStruct((2, HALF, 128), F32),
        ),
        in_specs=[hbm] * 4,
        out_specs=(vmem,) * 5,
        scratch_shapes=[
            pltpu.VMEM((2, STEPS, LROWS, HCOLS), jnp.bfloat16),
            pltpu.VMEM((1, LROWS), F32),
            pltpu.VMEM((HALF, 128), F32),
            pltpu.VMEM((2, PIECES, SROWS, 128), F32),
            pltpu.VMEM((PIECES, SROWS, 128), F32),
            pltpu.VMEM((PIECES, SROWS, 128), F32),
            pltpu.VMEM((NX + NZ, SROWS, 128), F32),
            pltpu.VMEM((NZ + NX, SROWS, 128), F32),
            pltpu.VMEM((NY, 1, 128), F32),
            pltpu.VMEM((2, PIECES, WROWS, 128), F32),
            pltpu.VMEM((PIECES, WROWS, 128), F32),
            pltpu.VMEM((PIECES, WROWS, 128), F32),
            pltpu.VMEM((NX + NZ, WROWS, 128), F32),
            pltpu.VMEM((2, PIECES, SROWS, 128), F32),
            pltpu.VMEM((NALL, 1, 128), F32),
            pltpu.VMEM((LOADED, 1, 128), F32),
            pltpu.VMEM((SENT, 1, 128), F32),
            two, dma, dma, dma, two, two, dma, dma, two, two, dma, dma, dma, regular, regular, regular,
        ],
        compiler_params=pltpu.CompilerParams(
            collective_id=0, has_side_effects=True, vmem_limit_bytes=40 * 2**20
        ),
        cost_estimate=pl.CostEstimate(flops=20_000_000, bytes_accessed=4_200_000, transcendentals=100_000),
    )(*[pltpu.with_memory_space_constraint(a, pltpu.HBM) for a in args])
    new_param, new_row, new_col = pl.pallas_call(
        finish,
        name="finish",
        out_shape=(
            jax.ShapeDtypeStruct((LROWS, LCOLS), F32),
            jax.ShapeDtypeStruct((1, LROWS), F32),
            jax.ShapeDtypeStruct((TILES, 128), F32),
        ),
        in_specs=[vmem] * 5,
        out_specs=(hbm,) * 3,
        scratch_shapes=[
            pltpu.VMEM((2, LROWS, HCOLS), F32),
            pltpu.VMEM((LROWS * TILES + TILES, 1, 128), F32),
            dma, dma,
        ],
        compiler_params=pltpu.CompilerParams(vmem_limit_bytes=40 * 2**20),
        cost_estimate=pl.CostEstimate(flops=2_000_000, bytes_accessed=1_200_000, transcendentals=0),
    )(*state)
    return new_param, new_row.reshape(LROWS), new_col.reshape(LCOLS)


def solution(mesh):
    placed = (P(None, "row", "col"), P("row", "col"), P("row"), P("col"))
    return jax.shard_map(
        local,
        mesh=mesh,
        in_specs=placed,
        out_specs=(P("row", "col"), P("row"), P("col")),
        check_vma=False,
    )
```

profile of v0, /device:TPU:1, one launch (start us, length us, event | category | flops | bytes accessed | tf_op | source)
XLA Modules:
  0.0 24.3 jit_solution(2164347539458720183)
XLA Ops:
  0.6 22.6 %exchange.1 = (f32[2,16,9216]{2,1,0:T(8,128)S(1)}, f32[2,3,16,9216]{3,2,1,0:T(8,128)S(1)}, f32[3,8,128]{2,1,0:T(8,128)S(1)}, f32[1,16]{1,0:T(1,128)S(1)}, f32[2,72,128]{2,1,0:T(8,128)S(1)}) custom-call(bf16[3,16,18432]{2,1,0:T(8,128)(2,1)} %grad_hbm.1, f32[16,18432]{1,0:T(8,128)} %param_hbm.1, f32[1,16]{1,0:T(1,128)} %bitcast.5, f32[144,128]{1,0:T(8,128)} %bitcast.4), custom_call_target="tpu_custom_call" | custom-call | flops 20000000 | bytes 4200000 | tf_op jit(solution)/shard_map/exchange/pallas_call | solution.py:388
  23.2 1.1 %finish.1 = (f32[16,18432]{1,0:T(8,128)}, f32[1,16]{1,0:T(1,128)}, f32[144,128]{1,0:T(8,128)}) custom-call(f32[2,16,9216]{2,1,0:T(8,128)S(1)} %get-tuple-element.11.p, f32[2,3,16,9216]{3,2,1,0:T(8,128)S(1)} %get-tuple-element.12.u, f32[3,8,128]{2,1,0:T(8,128)S(1)} %get-tuple-element.13.factor_ref, f32[1,16]{1,0:T(1,128)S(1)} %get-tuple-element.14.newrow_ref, ...), custom_call_target="tpu_custom_call" | custom-call | flops 2000000 | bytes 1200000 | tf_op jit(solution)/shard_map/finish/pallas_call | solution.py:425
where the time goes:
time: 24.4 us; the launch traced here: 24.3 us
  Pallas kernels  23.7 us (97%)
  between operations  0.64 us (3%)
    pallas_call x1, Pallas kernels, local(): pl.pallas_call(kernel, name='exchange', out_shape=(jax.ShapeDtypeStruct((...  22.6 us
    pallas_call x1, Pallas kernels, local(): pl.pallas_call(finish, name='finish', out_shape=(jax.ShapeDtypeStruct((LR...  1.06 us

commit v1 on v0

--- a/solution.py
+++ b/solution.py
@@ -26,7 +26,7 @@
 PRODUCTS = 6
 SENT = 2 * PIECES * SROWS + PIECES * WROWS + 6 * (3 * SROWS + WROWS) + NY - 1 + NALL - 1
 LOADED = LROWS * TILES + HALF
-OUT_PARTS = 3
+OUT_PARTS = 6
 
 
 def far_first():
@@ -374,7 +374,7 @@
                 o[h, :, cols] = a - (f[1] * u[h, 1, :, cols] + f[2] * u[h, 2, :, cols])
             src = o.at[h, :, pl.ds(part * width, width)]
             dst = out_hbm.at[:, pl.ds(pl.multiple_of(halves[h] * HCOLS + part * width, 128), width)]
-            pltpu.make_async_copy(src, dst, out_sem).start()
+            pltpu.make_async_copy(src, dst, out_sem).start(priority=part % 2)
     outs[0].wait()
     pltpu.make_async_copy(written, written, out_sem).wait()
 

time: 24.4 us -> 24.4 us (level)
  no operation moved by 1% of the time
where the time goes in v1:
time: 24.4 us; the launch traced here: 24.3 us
  Pallas kernels  23.6 us (97%)
  between operations  0.64 us (3%)
    pallas_call x1, Pallas kernels, local(): pl.pallas_call(kernel, name='exchange', out_shape=(jax.ShapeDtypeStruct((...  22.6 us
    pallas_call x1, Pallas kernels, local(): pl.pallas_call(finish, name='finish', out_shape=(jax.ShapeDtypeStruct((LR...  1.06 us

profile of v1, /device:TPU:1, one launch (start us, length us, event | category | flops | bytes accessed | tf_op | source)
XLA Modules:
  0.0 24.3 jit_solution(11456667835064375406)
XLA Ops:
  0.6 22.6 %exchange.1 = (f32[2,16,9216]{2,1,0:T(8,128)S(1)}, f32[2,3,16,9216]{3,2,1,0:T(8,128)S(1)}, f32[3,8,128]{2,1,0:T(8,128)S(1)}, f32[1,16]{1,0:T(1,128)S(1)}, f32[2,72,128]{2,1,0:T(8,128)S(1)}) custom-call(bf16[3,16,18432]{2,1,0:T(8,128)(2,1)} %grad_hbm.1, f32[16,18432]{1,0:T(8,128)} %param_hbm.1, f32[1,16]{1,0:T(1,128)} %bitcast.5, f32[144,128]{1,0:T(8,128)} %bitcast.4), custom_call_target="tpu_custom_call" | custom-call | flops 20000000 | bytes 4200000 | tf_op jit(solution)/shard_map/exchange/pallas_call | solution.py:388
  23.2 1.1 %finish.1 = (f32[16,18432]{1,0:T(8,128)}, f32[1,16]{1,0:T(1,128)}, f32[144,128]{1,0:T(8,128)}) custom-call(f32[2,16,9216]{2,1,0:T(8,128)S(1)} %get-tuple-element.11.p, f32[2,3,16,9216]{3,2,1,0:T(8,128)S(1)} %get-tuple-element.12.u, f32[3,8,128]{2,1,0:T(8,128)S(1)} %get-tuple-element.13.factor_ref, f32[1,16]{1,0:T(1,128)S(1)} %get-tuple-element.14.newrow_ref, ...), custom_call_target="tpu_custom_call" | custom-call | flops 2000000 | bytes 1200000 | tf_op jit(solution)/shard_map/finish/pallas_call | solution.py:425

commit v2 on v1

--- a/solution.py
+++ b/solution.py
@@ -252,11 +252,11 @@
     several(r1, 3, r1_r.at[0]).wait_recv()
     r2[z] = four(r1)
     for d in zs:
-        remote(r2.at[z], r2.at[z], r2_r, d).start()
+        remote(r2.at[z], r2.at[z], r2_r.at[0], d).start()
     several(r1, 3, r1_r.at[1]).wait_recv()
     r2[4 + x] = four(r1, 4)
     for d in xs:
-        remote(r2.at[4 + x], r2.at[4 + x], r2_r, d).start()
+        remote(r2.at[4 + x], r2.at[4 + x], r2_r.at[1], d).start()
 
     lax.fori_loop(0, 4, products(1), 0)
     wp_copies[0].wait_recv()
@@ -270,8 +270,8 @@
     scatter_z(w_sum, wr, wr_r.at[1])
 
     scale = []
-    several(r2, 6, r2_r).wait_recv()
     for axis, mine in ((0, x), (1, z + 4)):
+        several(r2, 3, r2_r.at[axis]).wait_recv()
         sums = four(r2, 4 * axis)
         first = mine * PTILES
         state8, state1 = col_ref[pl.ds(first, 8), :], col_ref[pl.ds(first + 8, 1), :]
@@ -415,7 +415,7 @@
             pltpu.VMEM((NALL, 1, 128), F32),
             pltpu.VMEM((LOADED, 1, 128), F32),
             pltpu.VMEM((SENT, 1, 128), F32),
-            two, dma, dma, dma, two, two, dma, dma, two, two, dma, dma, dma, regular, regular, regular,
+            two, dma, dma, dma, two, two, two, dma, two, two, dma, dma, dma, regular, regular, regular,
         ],
         compiler_params=pltpu.CompilerParams(
             collective_id=0, has_side_effects=True, vmem_limit_bytes=40 * 2**20

time: 24.4 us -> 24.4 us (level)
  no operation moved by 1% of the time
where the time goes in v2:
time: 24.4 us; the launch traced here: 24.3 us
  Pallas kernels  23.7 us (97%)
  between operations  0.64 us (3%)
    pallas_call x1, Pallas kernels, local(): pl.pallas_call(kernel, name='exchange', out_shape=(jax.ShapeDtypeStruct((...  22.6 us
    pallas_call x1, Pallas kernels, local(): pl.pallas_call(finish, name='finish', out_shape=(jax.ShapeDtypeStruct((LR...  1.06 us

profile of v2, /device:TPU:1, one launch (start us, length us, event | category | flops | bytes accessed | tf_op | source)
XLA Modules:
  0.0 24.3 jit_solution(10848662387838803016)
XLA Ops:
  0.6 22.6 %exchange.1 = (f32[2,16,9216]{2,1,0:T(8,128)S(1)}, f32[2,3,16,9216]{3,2,1,0:T(8,128)S(1)}, f32[3,8,128]{2,1,0:T(8,128)S(1)}, f32[1,16]{1,0:T(1,128)S(1)}, f32[2,72,128]{2,1,0:T(8,128)S(1)}) custom-call(bf16[3,16,18432]{2,1,0:T(8,128)(2,1)} %grad_hbm.1, f32[16,18432]{1,0:T(8,128)} %param_hbm.1, f32[1,16]{1,0:T(1,128)} %bitcast.5, f32[144,128]{1,0:T(8,128)} %bitcast.4), custom_call_target="tpu_custom_call" | custom-call | flops 20000000 | bytes 4200000 | tf_op jit(solution)/shard_map/exchange/pallas_call | solution.py:388
  23.2 1.1 %finish.1 = (f32[16,18432]{1,0:T(8,128)}, f32[1,16]{1,0:T(1,128)}, f32[144,128]{1,0:T(8,128)}) custom-call(f32[2,16,9216]{2,1,0:T(8,128)S(1)} %get-tuple-element.11.p, f32[2,3,16,9216]{3,2,1,0:T(8,128)S(1)} %get-tuple-element.12.u, f32[3,8,128]{2,1,0:T(8,128)S(1)} %get-tuple-element.13.factor_ref, f32[1,16]{1,0:T(1,128)S(1)} %get-tuple-element.14.newrow_ref, ...), custom_call_target="tpu_custom_call" | custom-call | flops 2000000 | bytes 1200000 | tf_op jit(solution)/shard_map/finish/pallas_call | solution.py:425
